TPU v7x, 256 devices: a whole 4x4x8 slice. The times are simulated.
256 devices in a mesh: tile: 32 (over z_lo, y, core), sample: 8 (over x, z_hi).
Axes of the slice: x: 4, y: 4, z: 8 (z_hi: 2, z_lo: 4; z = z_hi * 4 + z_lo), core: 2. Of those that a mesh axis runs over, the one named last changes fastest.
Arguments:
- inputs: bfloat16 [8, 16, 32, 1024], P('sample', None, 'tile'), may hold values from -6 to 6
- first_weight: bfloat16 [9, 1024, 1024], P(None, 'tile'), may hold values from -0.0625 to 0.0625
- second_weight: bfloat16 [9, 1024, 1024], P(None, 'tile'), may hold values from -0.0625 to 0.0625
- norm_gain_vector: float32 [1024], P('tile'), may hold values from 0.5 to 1.5
- norm_bias: float32 [1024], P('tile'), may hold values from -3 to 3
- cotangent: bfloat16 [8, 16, 32, 1024], P('sample', None, 'tile'), may hold values from -6 to 6
Outputs:
- input_grad: bfloat16 [8, 16, 32, 1024], P('sample', None, 'tile')
- first_grad: float32 [9, 1024, 1024], P(None, 'tile')
- second_grad: float32 [9, 1024, 1024], P(None, None, 'tile')
- gain_gradient: float32 [1024], P('tile')
- shift_grad: float32 [1024], P('tile')
All inputs are finite; a program needn't handle non-finite values.
Results may differ from a plain program's by a relative error of at most 0.0044.
Values may be sent and summed in bfloat16 or wider, within the bound.
No kernel may reach another device: no remote copies, remote signals or barrier semaphores. Data moves between devices by JAX's collectives and lax.ppermute only.
A program may use at most 64 MiB of HBM per device.

v0:
```python
import jax
import jax.numpy as jnp
from jax import lax
from jax.sharding import PartitionSpec as P

CHANNEL_COUNT = 1024
NORM_GROUPS = 32


OFFSETS = [(row_step, col_step) for row_step in (-1, 0, 1) for col_step in (-1, 0, 1)]


def shift_grid(block, row_step, col_step, row_axis):
    widths = [(0, 0)] * block.ndim
    widths[row_axis] = (1, 1)
    widths[row_axis + 1] = (1, 1)
    padded = jnp.pad(block, widths)
    height = block.shape[row_axis]
    across = block.shape[row_axis + 1]
    sliced = lax.slice_in_dim(padded, 1 + row_step, 1 + row_step + height, axis=row_axis)
    return lax.slice_in_dim(sliced, 1 + col_step, 1 + col_step + across, axis=row_axis + 1)


def contract(left, right, left_dim, right_dim):
    return lax.dot_general(
        left, right, (((left_dim,), (right_dim,)), ((), ())), preferred_element_type=jnp.float32
    )


def per_device(inputs, first_weight, second_weight, norm_gain_vector, norm_bias, cotangent):
    images, rows, col_local, width = inputs.shape
    group_fraction = first_weight.shape[1]
    gathered = lax.all_gather(inputs, "tile", axis=2, tiled=True)
    columns = gathered.shape[2]
    element_count = images * rows * columns
    chan_grid = (group_fraction, images, rows, columns)
    pre = jnp.zeros((group_fraction, element_count), jnp.float32)
    for tap, (row_step, col_step) in enumerate(OFFSETS):
        moved = shift_grid(gathered, row_step, col_step, 1).reshape(element_count, width)
        pre = pre + contract(first_weight[tap], moved, 1, 1)
    group_size = CHANNEL_COUNT // NORM_GROUPS
    per_dev = group_fraction // group_size
    group_view = pre.reshape(per_dev, group_size, images, rows * columns)
    group_mean = jnp.mean(group_view, axis=(1, 3), keepdims=True)
    variance = jnp.mean((group_view - group_mean) ** 2, axis=(1, 3), keepdims=True)
    inverse_deviation = lax.rsqrt(variance + 1e-05)
    input_groups = (group_view - group_mean) * inverse_deviation
    standardized_input = input_groups.reshape(group_fraction, element_count)
    normalized_output = standardized_input * norm_gain_vector[:, None] + norm_bias[:, None]
    sig = jax.nn.sigmoid(normalized_output)
    act = (normalized_output * sig).astype(jnp.bfloat16).reshape(chan_grid)
    first_cols, second_cols = (
        lax.all_to_all(first_weight, "tile", split_axis=2, concat_axis=1, tiled=True),
        lax.all_to_all(second_weight, "tile", split_axis=2, concat_axis=1, tiled=True),
    )
    dy_all = lax.all_gather(cotangent, "tile", axis=2, tiled=True)
    dy_rows = dy_all.reshape(element_count, width)
    second_grad = jnp.stack(
        [
            contract(
                dy_rows, shift_grid(act, rs, cs, 2).reshape(group_fraction, element_count), 0, 1
            )
            for rs, cs in OFFSETS
        ]
    )
    act_grad = jnp.zeros(chan_grid, jnp.float32)
    for tap, (row_step, col_step) in enumerate(OFFSETS):
        term = contract(second_cols[tap], dy_rows, 0, 1).reshape(chan_grid)
        act_grad = act_grad + shift_grid(term, -row_step, -col_step, 2)
    act_grad = act_grad.reshape(group_fraction, element_count)
    normed_gradient = act_grad * sig * (1.0 + normalized_output * (1.0 - sig))
    gain_gradient = jnp.sum(normed_gradient * standardized_input, axis=1)
    shift_grad = jnp.sum(normed_gradient, axis=1)
    scaled = (normed_gradient * norm_gain_vector[:, None]).reshape(
        per_dev, group_size, images, rows * columns
    )
    first_mean = jnp.mean(scaled, axis=(1, 3), keepdims=True)
    second_mean = jnp.mean(scaled * input_groups, axis=(1, 3), keepdims=True)
    pre_grad = (
        (inverse_deviation * (scaled - first_mean - input_groups * second_mean))
        .astype(jnp.bfloat16)
        .reshape(group_fraction, element_count)
    )
    first_grad = jnp.stack(
        [
            jnp.dot(
                pre_grad,
                shift_grid(gathered, rs, cs, 1).reshape(element_count, width),
                preferred_element_type=jnp.float32,
            )
            for rs, cs in OFFSETS
        ]
    )
    total = jnp.zeros(chan_grid, jnp.float32)
    piece = lax.all_gather(pre_grad.reshape(chan_grid), "tile", axis=0, tiled=True)
    width_piece = piece.shape[0]
    flat_piece = piece.reshape(width_piece, element_count)
    for tap, (back_row_step, back_col_step) in enumerate(OFFSETS):
        block = first_cols[tap]
        term = contract(block, flat_piece, 0, 0).reshape(chan_grid)
        total = total + shift_grid(term, -back_row_step, -back_col_step, 2)
    conv_back = total.astype(jnp.bfloat16)
    spatial = lax.all_to_all(conv_back, "tile", split_axis=3, concat_axis=0, tiled=True)
    spatial = jnp.transpose(spatial, (1, 2, 3, 0))
    input_grad = (cotangent.astype(jnp.float32) + spatial.astype(jnp.float32)).astype(jnp.bfloat16)
    first_grad, second_grad, gain_gradient, shift_grad = lax.psum(
        (first_grad, second_grad, gain_gradient, shift_grad), "sample"
    )
    return (input_grad, first_grad, second_grad, gain_gradient, shift_grad)


def solution(mesh):
    return jax.shard_map(
        per_device,
        mesh=mesh,
        in_specs=(
            P("sample", None, "tile", None),
            P(None, "tile", None),
            P(None, "tile", None),
            P("tile"),
            P("tile"),
            P("sample", None, "tile", None),
        ),
        out_specs=(
            P("sample", None, "tile", None),
            P(None, "tile", None),
            P(None, None, "tile"),
            P("tile"),
            P("tile"),
        ),
        check_vma=False,
    )
```

profile of v0, /device:TPU:32, one launch (start us, length us, event | category | flops | bytes accessed | tf_op | source)
XLA Modules:
  0.0 444.3 jit_solution(12824399923890636020)
XLA Ops:
  7.9 5.8 %copy.80 = bf16[9,32,1024]{1,0,2:T(8,128)(2,1)} copy(bf16[9,32,1024]{2,1,0:T(8,128)(2,1)} %param.8) | data formatting | bytes 1179648 | tf_op args[2]
  13.7 6.1 %reshape.415 = bf16[32,2,4608]{2,1,0:T(2,128)(2,1)} reshape(bf16[1024,9,32]{2,1,0:T(8,128)(2,1)} %bitcast.445) | data formatting | bytes 1179648
  19.8 8.9 %all-to-all-start = ((bf16[32,2,4608]{2,1,0:T(2,128)(2,1)}), bf16[32,2,4608]{2,1,0:T(2,128)(2,1)S(1)}, u32[]{:S(2)}, u32[]{:S(2)}) async-start(bf16[32,2,4608]{2,1,0:T(2,128)(2,1)} %reshape.415), calls=%async_computation | async-start | bytes 1179648 | tf_op jit(solution)/shard_map/all_to_all | solution.py:54
  28.7 4.7 %copy.88 = bf16[9,32,1024]{1,0,2:T(8,128)(2,1)} copy(bf16[9,32,1024]{2,1,0:T(8,128)(2,1)S(1)} %copy-done.10) | data formatting | bytes 1179648 | tf_op args[1]
  33.4 6.1 %reshape.417 = bf16[32,2,4608]{2,1,0:T(2,128)(2,1)} reshape(bf16[1024,9,32]{2,1,0:T(8,128)(2,1)} %bitcast.446) | data formatting | bytes 1179648
  39.5 6.1 %all-to-all-done = bf16[32,2,4608]{2,1,0:T(2,128)(2,1)S(1)} async-done(((bf16[32,2,4608]{2,1,0:T(2,128)(2,1)}), bf16[32,2,4608]{2,1,0:T(2,128)(2,1)S(1)}, u32[]{:S(2)}, u32[]{:S(2)}) %all-to-all-start) | async-done | bytes 589856 | tf_op jit(solution)/shard_map/all_to_all | solution.py:54
  45.6 6.5 %all-to-all-start.1 = ((bf16[32,2,4608]{2,1,0:T(2,128)(2,1)}), bf16[32,2,4608]{2,1,0:T(2,128)(2,1)S(1)}, u32[]{:S(2)}, u32[]{:S(2)}) async-start(bf16[32,2,4608]{2,1,0:T(2,128)(2,1)} %reshape.417), calls=%async_computation.1 | async-start | bytes 1179648 | tf_op jit(solution)/shard_map/all_to_all | solution.py:53
  53.2 3.8 reshape.416
  56.9 3.8 copy.189
  61.4 0.9 reshape.396
  62.3 0.9 reshape.395
  63.2 0.9 reshape.394
  64.1 0.9 reshape.393
  65.0 0.9 reshape.392
  65.9 0.9 reshape.391
  66.8 0.9 reshape.390
  67.7 0.9 reshape.389
  68.6 0.9 reshape.388
  69.5 3.7 reshape.418
  73.2 3.8 copy.188
  78.0 0.9 squeeze.106
  78.9 0.9 squeeze.105
  79.8 0.9 squeeze.104
  80.7 0.9 squeeze.103
  81.6 0.9 squeeze.102
  82.5 0.9 squeeze.101
  83.4 0.9 squeeze.100
  84.3 0.9 squeeze.99
  85.2 1.8 copy.78
  87.0 4.0 pad_slice_fusion
  94.7 1.0 fusion.132
  98.6 35.9 %all-gather.6.cloned.1.call-done = bf16[1,16,32,1024]{3,1,0,2:T(8,128)(2,1)} async-done(((bf16[1,16,1,1024]{3,1,0,2:T(8,128)(2,1)}), bf16[1,16,32,1024]{3,1,0,2:T(8,128)(2,1)}) %all-gather.6.cloned.1.call-update) | async-done | bytes 1048592 | tf_op jit(solution)/shard_map/all_gather | solution.py:56
  134.5 2.3 convolution_bitcast_fusion.8
  136.8 1.0 convolution_bitcast_fusion.7
  137.8 1.0 convolution_bitcast_fusion.6
  138.8 1.0 convolution_bitcast_fusion.5
  139.8 1.0 convolution_bitcast_fusion.3
  140.8 1.0 convolution_bitcast_fusion.2
  141.8 1.0 convolution_bitcast_fusion.1
  142.8 1.0 convolution_bitcast_fusion
  143.8 1.9 multiply_reduce_fusion
  145.9 0.8 reshape.366
  146.7 1.6 multiply_reduce_fusion.1
  149.6 2.2 fusion.13
  151.9 0.8 reshape_reshape.3
  152.8 2.2 fusion.12
  155.2 2.0 fusion.22
  159.5 0.8 fusion.18
  163.2 1.0 fusion.11
  164.2 0.9 fusion.10
  165.2 0.9 fusion.9
  166.1 0.9 fusion.8
  167.1 0.9 fusion.7
  168.0 0.9 fusion.6
  169.0 0.9 fusion.5
  170.0 47.3 %all-gather.8.cloned.1.call-done = bf16[1024,1,16,32]{3,2,1,0:T(8,128)(2,1)} async-done(((bf16[32,1,16,32]{3,2,1,0:T(8,128)(2,1)}), bf16[1024,1,16,32]{3,2,1,0:T(8,128)(2,1)}) %all-gather.8.cloned.1.call-update) | async-done | bytes 1048592 | tf_op jit(solution)/shard_map/all_gather | solution.py:95
  217.3 4.6 %copy.87 = bf16[1024,1,16,32]{0,3,2,1:T(8,128)(2,1)S(1)} copy(bf16[1024,1,16,32]{3,2,1,0:T(8,128)(2,1)} %all-gather.8.cloned.1.call-done) | data formatting | bytes 2097152 | tf_op jit(solution)/shard_map/all_gather | solution.py:95
  229.4 0.8 reshape.419
  230.1 5.7 %all-to-all-start.2 = ((bf16[32,2,256]{2,1,0:T(2,128)(2,1)}), bf16[32,2,256]{2,1,0:T(2,128)(2,1)S(1)}, u32[]{:S(2)}, u32[]{:S(2)}) async-start(bf16[32,2,256]{2,1,0:T(2,128)(2,1)} %reshape.419), calls=%async_computation.2 | async-start | bytes 65536 | tf_op jit(solution)/shard_map/all_to_all | solution.py:103
  235.8 36.2 %all-reduce.18 = (f32[32]{0:T(128)}, f32[32]{0:T(128)}) all-reduce(f32[32]{0:T(128)S(1)} %get-tuple-element.5, f32[32]{0:T(128)S(1)} %get-tuple-element.41), channel_id=1, replica_groups=mesh['tile'=32,'sample'=8] {'sample'}, use_global_device_ids=true, to_apply=%region_7.8 | all-reduce | flops 64 | bytes 512 | tf_op jit(solution)/shard_map/psum | solution.py:106
  272.1 53.4 %all-to-all-done.2 = bf16[32,2,256]{2,1,0:T(2,128)(2,1)S(1)} async-done(((bf16[32,2,256]{2,1,0:T(2,128)(2,1)}), bf16[32,2,256]{2,1,0:T(2,128)(2,1)S(1)}, u32[]{:S(2)}, u32[]{:S(2)}) %all-to-all-start.2) | async-done | bytes 32800 | tf_op jit(solution)/shard_map/all_to_all | solution.py:103
  326.5 107.5 %all-reduce.22.cloned.1.call-done = (f32[9,32,1024]{2,1,0:T(8,128)}, f32[9,1024,32]{1,2,0:T(8,128)}) async-done(((f32[9,32,1024]{2,1,0:T(8,128)}, f32[9,1024,32]{1,2,0:T(8,128)}), (f32[9,32,1024]{2,1,0:T(8,128)}, f32[9,1024,32]{1,2,0:T(8,128)})) %all-reduce.22.cloned.1.call-update) | async-done | bytes 2359312 | tf_op jit(solution)/shard_map/psum | solution.py:106
  434.0 2.5 copy.208
  436.5 1.0 copy.209
  (141 shorter events, 22.3 us)
Async XLA Ops:
  7.2 78.0 %all-gather.4.cloned.1.call-start = ((), (), s32[]{:S(2)}) async-start(), calls=%async_computation.3 | async-start | bytes 1081344 | tf_op jit(solution)/shard_map/all_gather | solution.py:33
  19.8 8.9 %copy-start.10 = (bf16[9,32,1024]{2,1,0:T(8,128)(2,1)S(1)}, bf16[9,32,1024]{2,1,0:T(8,128)(2,1)}, u32[]{:S(2)}) copy-start(bf16[9,32,1024]{2,1,0:T(8,128)(2,1)} %param.7) | copy-start | bytes 1769476
  19.8 25.8 %all-to-all-start = ((bf16[32,2,4608]{2,1,0:T(2,128)(2,1)}), bf16[32,2,4608]{2,1,0:T(2,128)(2,1)S(1)}, u32[]{:S(2)}, u32[]{:S(2)}) async-start(bf16[32,2,4608]{2,1,0:T(2,128)(2,1)} %reshape.415), calls=%async_computation | async-start | bytes 1179648 | tf_op jit(solution)/shard_map/all_to_all | solution.py:54
  45.6 23.9 %all-to-all-start.1 = ((bf16[32,2,4608]{2,1,0:T(2,128)(2,1)}), bf16[32,2,4608]{2,1,0:T(2,128)(2,1)S(1)}, u32[]{:S(2)}, u32[]{:S(2)}) async-start(bf16[32,2,4608]{2,1,0:T(2,128)(2,1)} %reshape.417), calls=%async_computation.1 | async-start | bytes 1179648 | tf_op jit(solution)/shard_map/all_to_all | solution.py:53
  52.1 82.4 %all-gather.6.cloned.1.call-start = ((), (), s32[]{:S(2)}) async-start(), calls=%async_computation.4 | async-start | bytes 1081344 | tf_op jit(solution)/shard_map/all_gather | solution.py:56
  52.8 164.5 %all-gather.8.cloned.1.call-start = ((), (), s32[]{:S(2)}) async-start(), calls=%async_computation.5 | async-start | bytes 4325376 | tf_op jit(solution)/shard_map/all_gather | solution.py:95
  87.0 4.1 copy-start.11
  91.0 1.4 copy-start.4
  91.0 2.2 copy-start.2
  91.1 2.6 copy-start.6
  91.1 2.6 copy-start.8
  91.1 2.6 copy-start.9
  91.1 2.7 copy-start
  94.2 3.5 copy-start.32
  94.3 3.4 copy-start.33
  134.5 2.3 copy-start.31
  134.5 2.3 copy-start.34
  134.5 3.3 copy-start.30
  136.8 2.0 copy-start.29
  137.8 2.0 copy-start.28
  138.8 2.0 copy-start.27
  139.8 2.0 copy-start.26
  140.8 2.0 copy-start.24
  141.8 2.0 copy-start.25
  146.7 6.0 %copy-start.22 = (bf16[32,512]{1,0:T(8,128)(2,1)S(1)}, bf16[32,512]{1,0:T(8,128)(2,1)}, u32[]{:S(2)}) copy-start(bf16[32,512]{1,0:T(8,128)(2,1)} %get-tuple-element.12) | copy-start | bytes 98308
  149.6 5.6 %copy-start.36 = (bf16[32,1,16,32]{3,0,2,1:T(8,128)(2,1)S(1)}, bf16[32,1,16,32]{3,0,2,1:T(8,128)(2,1)}, u32[]{:S(2)}) copy-start(bf16[32,1,16,32]{3,0,2,1:T(8,128)(2,1)} %get-tuple-element.42) | copy-start | bytes 98308
  155.0 279.0 %all-reduce.22.cloned.1.call-start = ((), (), s32[]{:S(2)}) async-start(), calls=%async_computation.6 | async-start | bytes 4718592 | tf_op jit(solution)/shard_map/psum | solution.py:106
  155.2 2.1 copy-start.35
  161.7 1.5 copy-start.7
  162.4 1.8 copy-start.5
  163.2 2.0 copy-start.13
  164.2 1.9 copy-start.3
  165.2 1.9 copy-start.1
  170.0 51.9 %copy-start.19 = (bf16[1024,32]{0,1:T(8,128)(2,1)S(1)}, bf16[1024,32]{0,1:T(8,128)(2,1)}, u32[]{:S(2)}) copy-start(bf16[1024,32]{0,1:T(8,128)(2,1)} %squeeze.101) | copy-start | bytes 196612
  221.9 0.8 copy-start.20
  221.9 1.2 copy-start.21
  223.7 0.9 copy-start.18
  224.4 1.0 copy-start.17
  225.1 1.0 copy-start.16
  225.9 1.0 copy-start.15
  226.6 1.0 copy-start.14
  229.4 96.5 %copy-start.23 = (bf16[1,16,1,1024]{3,1,2,0:T(8,128)(2,1)S(1)}, bf16[1,16,1,1024]{3,1,2,0:T(8,128)(2,1)}, u32[]{:S(2)}) copy-start(bf16[1,16,1,1024]{3,1,2,0:T(8,128)(2,1)} %param.11) | copy-start | bytes 98308
  230.1 95.3 %all-to-all-start.2 = ((bf16[32,2,256]{2,1,0:T(2,128)(2,1)}), bf16[32,2,256]{2,1,0:T(2,128)(2,1)S(1)}, u32[]{:S(2)}, u32[]{:S(2)}) async-start(bf16[32,2,256]{2,1,0:T(2,128)(2,1)} %reshape.419), calls=%async_computation.2 | async-start | bytes 65536 | tf_op jit(solution)/shard_map/all_to_all | solution.py:103
  434.0 2.5 copy-start.12
Sparse Core Ops, SparseCore 0:
  9.9 64.3 all-gather.3
  76.1 58.3 all-gather.5
  155.1 62.1 all-gather.7
  220.4 213.5 all-reduce.21
where the time goes:
time: 451 us; the launch traced here: 444 us
  waiting for transfers between devices  252 us (56%)
  local copies, waits for them, and re-layouts  75.3 us (17%)
  matrix products  38.1 us (8%)
  blocking collectives  36.2 us (8%)
  starting transfers between devices  21.7 us (5%)
  between operations  17.4 us (4%)
    psum x1, waiting for transfers between devices, per_device(): lax.psum((first_grad, second_grad, gain_gradient, shift_grad), 'sample')  108 us
    all_to_all x1, waiting for transfers between devices, per_device(): lax.all_to_all(conv_back, 'tile', split_axis=3, concat_axis=0, tiled=True)  53.4 us
    all_gather x1, waiting for transfers between devices, per_device(): lax.all_gather(pre_grad.reshape(chan_grid), 'tile', axis=0, tiled=True)  47.3 us
    psum x1, blocking collectives, per_device(): lax.psum((first_grad, second_grad, gain_gradient, shift_grad), 'sample')  36.2 us
    all_gather x1, waiting for transfers between devices, per_device(): dy_all = lax.all_gather(cotangent, 'tile', axis=2, tiled=True)  35.9 us
    unnamed x84, local copies, waits for them, and re-layouts  35.4 us
    dot_general x36, matrix products, contract(): lax.dot_general(left, right, (((left_dim,), (right_dim,)), ((), ())), pre...  27 us
    dot_general x9, matrix products, per_device(): jnp.dot(pre_grad, shift_grid(gathered, rs, cs, 1).reshape(element_count,...  11.1 us
  transfers between devices with their start and end apart: 7, of which 5 were waited for; matrix products, arithmetic and copies ran while one was open for 21% of the time, Pallas kernels for 0%

commit v1 on v0

v1 whole, which is shorter than its diff:
```python
import functools

import jax
import jax.numpy as jnp
from jax import lax
from jax.experimental import pallas as pl
from jax.experimental.pallas import tpu as pltpu
from jax.sharding import PartitionSpec as P

BF = jnp.bfloat16
F32 = jnp.float32
TAPS = [(dr, dc) for dr in (-1, 0, 1) for dc in (-1, 0, 1)]
ROWS, COLS, CH = 16, 32, 1024
POS = ROWS * COLS
OWN = 32
MB = 1 << 20

Z_MASKS, Y_MASKS, CORE = (8, 16, 24), (2, 4, 6), 1
ORDER = [c ^ y ^ z for c in (0, 1) for y in (0, 2, 4, 6) for z in (0, 8, 16, 24)]
SUM_ORDER = [c ^ y ^ z for c in (0, 1) for y in (0, 2, 4, 6) for z in (0, 8, 16, 24)]


def hop(value, mask, axis="tile", size=32):
    return lax.ppermute(value, axis, [(i, i ^ mask) for i in range(size)])


def gather_columns(block):
    held = block[None]
    for masks in (Z_MASKS, Y_MASKS):
        held = jnp.concatenate([held] + [hop(held, m) for m in masks], axis=0)
    return held, hop(held, CORE)


def shifted(value, dr, dc):
    step = ROWS * dc + dr
    moved = pltpu.roll(value, (-step) % POS, 1) if step else value
    if step == 0:
        return moved
    place = lax.broadcasted_iota(jnp.int32, value.shape, 1)
    row, col = place % ROWS + dr, place // ROWS + dc
    inside = (row >= 0) & (row < ROWS) & (col >= 0) & (col < COLS)
    return jnp.where(inside, moved, 0.0)


def assemble(me, near_ref, far_ref, out_ref):
    half = len(ORDER) // 2
    for k, mask in enumerate(ORDER):
        col = me ^ mask
        src = near_ref if k < half else far_ref
        out_ref[pl.ds(pl.multiple_of(col * ROWS, ROWS), ROWS), :] = src[k % half]


def dot(a, b, ca, cb):
    return lax.dot_general(a, b, (((ca,), (cb,)), ((), ())), preferred_element_type=F32)


def forward_kernel(me_ref, near_ref, far_ref, w_ref, gain_ref, bias_ref, x_ref, taps_ref, xhat_ref, slope_ref, rstd_ref):
    assemble(me_ref[0], near_ref, far_ref, x_ref)
    products = dot(w_ref[...], x_ref[...], 1, 1)
    pre = jnp.zeros((OWN, POS), F32)
    for t, (dr, dc) in enumerate(TAPS):
        pre = pre + shifted(products[OWN * t : OWN * (t + 1)], dr, dc)
    count = 1.0 / (OWN * POS)
    mean = jnp.sum(pre, keepdims=True) * count
    centred = pre - mean
    rstd = lax.rsqrt(jnp.sum(centred * centred, keepdims=True) * count + 1e-05)
    xhat = centred * rstd
    normed = xhat * gain_ref[...] + bias_ref[...]
    sig = jax.nn.sigmoid(normed)
    act = (normed * sig).astype(BF).astype(F32)
    for t, (dr, dc) in enumerate(TAPS):
        taps_ref[OWN * t : OWN * (t + 1), :] = shifted(act, dr, dc).astype(BF)
    xhat_ref[...] = xhat
    slope_ref[...] = sig * (1.0 + normed * (1.0 - sig))
    rstd_ref[...] = jnp.broadcast_to(rstd, rstd_ref.shape)


def split_blocks(xi, grad, whole_ref, outs):
    whole_ref[...] = grad
    rows = grad.shape[0]
    for m, out in enumerate(outs):
        lane = pl.multiple_of((xi ^ m) * 256, 256)
        out[:rows, :] = whole_ref[:, pl.ds(lane, 256)].astype(out.dtype)


def second_kernel(me_ref, near_ref, far_ref, taps_ref, dy_ref, g0, g1, g2, g3, whole_ref):
    assemble(me_ref[0], near_ref, far_ref, dy_ref)
    split_blocks(me_ref[1], dot(taps_ref[...], dy_ref[...], 1, 0), whole_ref, (g0, g1, g2, g3))


def turn_kernel(w_ref, out_ref):
    out_ref[:, : 9 * OWN] = w_ref[...].astype(F32).T.astype(BF)
    out_ref[:, 9 * OWN :] = jnp.zeros((CH, 96), BF)


def backward_kernel(
    me_ref, w2_ref, dy_ref, x_ref, w1_ref, gain_ref, xhat_ref, slope_ref, rstd_ref,
    p_near, p_far, g0, g1, g2, g3, w2t_ref, whole_ref, taps_ref, rows_ref,
):
    me = me_ref[0]
    for t in range(9):
        base, at = 128 * (t // 4), OWN * (t % 4)
        for g in range(8):
            parts = [w2_ref[4 * g + j][:, base + at : base + at + OWN].astype(F32) for j in range(4)]
            w2t_ref[OWN * t : OWN * (t + 1), 128 * g : 128 * (g + 1)] = jnp.concatenate(parts, axis=1).astype(BF)
    products = dot(w2t_ref[...], dy_ref[...], 1, 1)
    act_grad = jnp.zeros((OWN, POS), F32)
    for t, (dr, dc) in enumerate(TAPS):
        act_grad = act_grad + shifted(products[OWN * t : OWN * (t + 1)], -dr, -dc)
    xhat = xhat_ref[...]
    norm_grad = act_grad * slope_ref[...]
    gain_sum = jnp.sum(norm_grad * xhat, axis=1, keepdims=True)
    shift_sum = jnp.sum(norm_grad, axis=1, keepdims=True)
    scaled = norm_grad * gain_ref[...]
    count = 1.0 / (OWN * POS)
    first_mean = jnp.sum(scaled, keepdims=True) * count
    second_mean = jnp.sum(scaled * xhat, keepdims=True) * count
    pre_grad = rstd_ref[0:1, 0:1] * (scaled - first_mean - xhat * second_mean)
    pre_grad = pre_grad.astype(BF).astype(F32)
    for t, (dr, dc) in enumerate(TAPS):
        taps_ref[OWN * t : OWN * (t + 1), :] = shifted(pre_grad, -dr, -dc)
    taps = taps_ref[...]
    split_blocks(me_ref[1], dot(taps.astype(BF), x_ref[...], 1, 0), whole_ref, (g0, g1, g2, g3))
    high_g = gain_sum.astype(BF).astype(F32)
    high_s = shift_sum.astype(BF).astype(F32)
    lane = lax.broadcasted_iota(jnp.int32, (OWN, 128), 1)
    sums = jnp.where(lane == 0, high_g, 0.0) + jnp.where(lane == 1, gain_sum - high_g, 0.0)
    sums = sums + jnp.where(lane == 2, high_s, 0.0) + jnp.where(lane == 3, shift_sum - high_s, 0.0)
    extra = sums.T[:16, :]
    for out in (g0, g1, g2, g3):
        out[9 * OWN :, :] = jnp.zeros((16, 256), out.dtype)
        out[9 * OWN :, :OWN] = extra.astype(out.dtype)
    rows_ref[...] = taps.T
    half = len(SUM_ORDER) // 2
    for part, out in enumerate((p_near, p_far)):
        blocks = []
        for mask in SUM_ORDER[part * half : (part + 1) * half]:
            start = pl.multiple_of((me ^ mask) * ROWS, ROWS)
            blocks.append(rows_ref[pl.ds(start, ROWS), :])
        out[...] = dot(jnp.concatenate(blocks, axis=0).astype(BF), w1_ref[...], 1, 0)


def finish_kernel(me_ref, a0, a1, a2, a3, out_ref):
    for m, part in enumerate((a0, a1, a2, a3)):
        lane = pl.multiple_of((me_ref[1] ^ m) * 256, 256)
        out_ref[:, pl.ds(lane, 256)] = part[: 9 * OWN, :].astype(F32)


def call(kernel, outs, scratch=(), n_in=1, flops=0):
    smem = pl.BlockSpec(memory_space=pltpu.SMEM)
    vmem = pl.BlockSpec(memory_space=pltpu.VMEM)
    return pl.pallas_call(
        kernel,
        out_shape=[jax.ShapeDtypeStruct(s, d) for s, d in outs],
        in_specs=[smem] + [vmem] * n_in,
        out_specs=[vmem] * len(outs),
        scratch_shapes=[pltpu.VMEM(s, d) for s, d in scratch],
        compiler_params=pltpu.CompilerParams(vmem_limit_bytes=32 * MB),
        cost_estimate=pl.CostEstimate(flops=flops, bytes_accessed=4 * MB, transcendentals=0),
    )


def sum_over_sample(parts):
    total = parts[0]
    got = [hop(parts[m], 2 * m, "sample", 8) for m in (1, 2, 3)]
    for r in got:
        total = total + r.astype(F32)
    mine = total.astype(BF)
    mine = (mine.astype(F32) + hop(mine, 1, "sample", 8).astype(F32)).astype(BF)
    return [mine] + [hop(mine, 2 * m, "sample", 8) for m in (1, 2, 3)]


def per_device(inputs, first_weight, second_weight, norm_gain_vector, norm_bias, cotangent):
    tile = lax.axis_index("tile").astype(jnp.int32)
    place = jnp.stack([tile, (lax.axis_index("sample") // 2).astype(jnp.int32)])
    x_near, x_far = gather_columns(inputs.reshape(ROWS, CH))
    dy_near, dy_far = gather_columns(cotangent.reshape(ROWS, CH))
    w1 = first_weight.reshape(9 * OWN, CH)
    w2 = second_weight.reshape(9 * OWN, CH)
    gain, bias = norm_gain_vector[:, None], norm_bias[:, None]
    vmem = pl.BlockSpec(memory_space=pltpu.VMEM)
    turned = pl.pallas_call(
        turn_kernel,
        out_shape=jax.ShapeDtypeStruct((CH, 384), BF),
        in_specs=[vmem],
        out_specs=vmem,
        compiler_params=pltpu.CompilerParams(vmem_limit_bytes=32 * MB),
    )(w2)
    w2_own = lax.all_to_all(turned.reshape(32, OWN, 384), "tile", split_axis=0, concat_axis=0, tiled=True)
    flops = 2 * 288 * POS * CH
    x_all, act_taps, xhat, slope, rstd = call(
        forward_kernel,
        [((POS, CH), BF), ((9 * OWN, POS), BF), ((OWN, POS), F32), ((OWN, POS), F32), ((8, 128), F32)],
        n_in=5, flops=flops,
    )(place, x_near, x_far, w1, gain, bias)
    blocks = [((9 * OWN, 256), F32)] + [((9 * OWN, 256), BF)] * 3
    whole = [((9 * OWN, CH), F32)]
    dy_all, *second_parts = call(second_kernel, [((POS, CH), BF)] + blocks, whole, n_in=3, flops=flops)(
        place, dy_near, dy_far, act_taps
    )
    blocks = [((9 * OWN + 16, 256), F32)] + [((9 * OWN + 16, 256), BF)] * 3
    near, far, *first_parts = call(
        backward_kernel,
        [((POS // 2, CH), F32)] * 2 + blocks,
        [((9 * OWN, CH), BF)] + whole + [((9 * OWN, POS), F32), ((POS, 9 * OWN), F32)],
        n_in=8, flops=3 * flops,
    )(place, w2_own, dy_all, x_all, w1, gain, xhat, slope, rstd)
    total = (near + hop(far, CORE)).reshape(4, POS // 8, CH)
    got = [hop(total[k].astype(BF), m) for k, m in zip((1, 2, 3), Y_MASKS)]
    total = total[0] + got[0].astype(F32) + got[1].astype(F32) + got[2].astype(F32)
    total = total.reshape(4, ROWS, CH)
    got = [hop(total[k], m) for k, m in zip((1, 2, 3), Z_MASKS)]
    total = total[0] + got[0] + got[1] + got[2]
    conv_back = total.astype(BF).astype(F32)
    input_grad = (cotangent.reshape(ROWS, CH).astype(F32) + conv_back).astype(BF)
    second = sum_over_sample(second_parts)
    first = sum_over_sample(first_parts)
    (second_grad,) = call(finish_kernel, [((9 * OWN, CH), F32)], n_in=4)(place, *second)
    (first_grad,) = call(finish_kernel, [((9 * OWN, CH), F32)], n_in=4)(place, *first)
    xi = place[1]
    extras = jnp.stack([p[9 * OWN : 9 * OWN + 4, :OWN] for p in first]).astype(F32)
    sums = lax.dynamic_index_in_dim(extras, xi, 0, keepdims=False)
    return (
        input_grad.reshape(1, ROWS, 1, CH),
        first_grad.reshape(9, OWN, CH),
        jnp.transpose(second_grad.reshape(9, OWN, CH), (0, 2, 1)),
        sums[0] + sums[1],
        sums[2] + sums[3],
    )


def solution(mesh):
    return jax.shard_map(
        per_device,
        mesh=mesh,
        in_specs=(
            P("sample", None, "tile", None),
            P(None, "tile", None),
            P(None, "tile", None),
            P("tile"),
            P("tile"),
            P("sample", None, "tile", None),
        ),
        out_specs=(
            P("sample", None, "tile", None),
            P(None, "tile", None),
            P(None, None, "tile"),
            P("tile"),
            P("tile"),
        ),
        check_vma=False,
    )
```

time: 451 us -> 133 us (0.29); the launches traced: 444 us -> 131 us
  waiting for transfers between devices: 252 us -> 39.5 us
  local copies, waits for them, and re-layouts: 75.3 us -> 10.8 us
  starting transfers between devices: 21.7 us -> 64.3 us
  matrix products: 38.1 us -> 0 us
  blocking collectives: 36.2 us -> 0 us
  between operations: 17.4 us -> 0.98 us
  Pallas kernels: 0 us -> 12.6 us
    psum x1 -> x0, waiting for transfers between devices: 108 us -> none  [per_device(): lax.psum((first_grad, second_grad, gain_gradient, shift_grad), 'sample')]
    all_gather x3 -> x0, waiting for transfers between devices: 83.3 us -> none  [the longest x1 47.3 us: per_device(): lax.all_gather(pre_grad.reshape(chan_grid), 'tile', axis=0, tiled=True)]
    all_to_all x3 -> x1, waiting for transfers between devices: 59.4 us -> 0.01 us  [per_device(): lax.all_to_all(turned.reshape(32, OWN, 384), 'tile', split_axis=0, concat...]
    ppermute x0 -> x35, starting transfers between devices: none -> 57.7 us  [hop(): return lax.ppermute(value, axis, [(i, i ^ mask) for i in range(size)])]
    ppermute x0 -> x35, waiting for transfers between devices: none -> 39.5 us  [hop(): return lax.ppermute(value, axis, [(i, i ^ mask) for i in range(size)])]
    dot_general x45 -> x0, matrix products: 38.1 us -> none  [the longest x36 27 us: contract(): lax.dot_general(left, right, (((left_dim,), (right_dim,)), ((), ())), pre...]
    psum x1 -> x0, blocking collectives: 36.2 us -> none  [per_device(): lax.psum((first_grad, second_grad, gain_gradient, shift_grad), 'sample')]
    unnamed x84 -> x54, local copies, waits for them, and re-layouts: 35.4 us -> 9.93 us
  transfers between devices with their start and end apart: 7 -> 36, of which waited for: 5 -> 14; matrix products, arithmetic and copies ran while one was open for 21% -> 2% of each run, Pallas kernels for 0% -> 10%
where the time goes in v1:
time: 133 us; the launch traced here: 131 us
  starting transfers between devices  64.3 us (48%)
  waiting for transfers between devices  39.5 us (30%)
  Pallas kernels  12.6 us (9%)
  local copies, waits for them, and re-layouts  10.8 us (8%)
  other arithmetic  2.83 us (2%)
    ppermute x35, starting transfers between devices, hop(): return lax.ppermute(value, axis, [(i, i ^ mask) for i in range(size)])  57.7 us
    ppermute x35, waiting for transfers between devices, hop(): return lax.ppermute(value, axis, [(i, i ^ mask) for i in range(size)])  39.5 us
    unnamed x54, local copies, waits for them, and re-layouts  9.93 us
    all_to_all x1, starting transfers between devices, per_device(): lax.all_to_all(turned.reshape(32, OWN, 384), 'tile', split_axis=0, concat...  6.65 us
    pallas_call x1, Pallas kernels, per_device(): call(backward_kernel, [((POS // 2, CH), F32)] * 2 + blocks, [((9 * OWN, C...  4.1 us
  transfers between devices with their start and end apart: 36, of which 14 were waited for; matrix products, arithmetic and copies ran while one was open for 2% of the time, Pallas kernels for 10%

profile of v1, /device:TPU:32, one launch (start us, length us, event | category | flops | bytes accessed | tf_op | source)
XLA Modules:
  0.0 131.1 jit_solution(2785410135439681307)
XLA Ops:
  0.6 1.9 %collective-permute-start.7 = (bf16[1,16,1024]{2,1,0:T(8,128)(2,1)}, bf16[1,16,1024]{2,1,0:T(8,128)(2,1)S(1)}, u32[]{:S(2)}, u32[]{:S(2)}) collective-permute-start(bf16[1,16,1024]{2,1,0:T(8,128)(2,1)} %bitcast.41), channel_id=1, source_target_pairs={{0,64},{8,72},{16,80},{24,88},{32,96},{40,104},{48,112},{56,120},{... | collective-permute-start | bytes 98312 | tf_op jit(solution)/shard_map/ppermute | solution.py:24
  2.6 1.5 %collective-permute-start.8 = (bf16[1,16,1024]{2,1,0:T(8,128)(2,1)}, bf16[1,16,1024]{2,1,0:T(8,128)(2,1)S(1)}, u32[]{:S(2)}, u32[]{:S(2)}) collective-permute-start(bf16[1,16,1024]{2,1,0:T(8,128)(2,1)} %bitcast.42), channel_id=1, source_target_pairs={{0,128},{8,136},{16,144},{24,152},{32,160},{40,168},{48,176},{56,1... | collective-permute-start | bytes 98312 | tf_op jit(solution)/shard_map/ppermute | solution.py:24
  4.1 0.5 collective-permute-start.9
  4.6 2.4 %collective-permute-start = (bf16[1,16,1024]{2,1,0:T(8,128)(2,1)}, bf16[1,16,1024]{2,1,0:T(8,128)(2,1)S(1)}, u32[]{:S(2)}, u32[]{:S(2)}) collective-permute-start(bf16[1,16,1024]{2,1,0:T(8,128)(2,1)} %bitcast.37), channel_id=1, source_target_pairs={{0,64},{8,72},{16,80},{24,88},{32,96},{40,104},{48,112},{56,120},{... | collective-permute-start | bytes 98312 | tf_op jit(solution)/shard_map/ppermute | solution.py:24
  7.0 1.4 %collective-permute-start.1 = (bf16[1,16,1024]{2,1,0:T(8,128)(2,1)}, bf16[1,16,1024]{2,1,0:T(8,128)(2,1)S(1)}, u32[]{:S(2)}, u32[]{:S(2)}) collective-permute-start(bf16[1,16,1024]{2,1,0:T(8,128)(2,1)} %bitcast.38), channel_id=1, source_target_pairs={{0,128},{8,136},{16,144},{24,152},{32,160},{40,168},{48,176},{56,1... | collective-permute-start | bytes 98312 | tf_op jit(solution)/shard_map/ppermute | solution.py:24
  8.4 1.1 copy-done.3
  9.4 1.2 shard_map.101
  10.6 6.6 %all-to-all-start = ((bf16[32,32,384]{2,1,0:T(8,128)(2,1)}), bf16[32,32,384]{2,1,0:T(8,128)(2,1)S(1)}, u32[]{:S(2)}, u32[]{:S(2)}) async-start(bf16[32,32,384]{2,1,0:T(8,128)(2,1)} %bitcast.4), calls=%async_computation | async-start | bytes 1572864 | tf_op jit(solution)/shard_map/all_to_all | solution.py:189
  17.3 1.6 %collective-permute-start.2 = (bf16[1,16,1024]{2,1,0:T(8,128)(2,1)S(1)}, bf16[1,16,1024]{2,1,0:T(8,128)(2,1)S(1)}, u32[]{:S(2)}, u32[]{:S(2)}) collective-permute-start(bf16[1,16,1024]{2,1,0:T(8,128)(2,1)S(1)} %bitcast.39), channel_id=1, source_target_pairs={{0,192},{8,200},{16,208},{24,216},{32,224},{40,232},{48,240},{56,2... | collective-permute-start | bytes 98312 | tf_op jit(solution)/shard_map/ppermute | solution.py:24
  18.9 1.6 %collective-permute-start.10 = (bf16[4,16,1024]{2,1,0:T(8,128)(2,1)S(1)}, bf16[4,16,1024]{2,1,0:T(8,128)(2,1)S(1)}, u32[]{:S(2)}, u32[]{:S(2)}) collective-permute-start(bf16[4,16,1024]{2,1,0:T(8,128)(2,1)S(1)} %pad_maximum_fusion.1), channel_id=1, source_target_pairs={{0,16},{8,24},{16,0},{24,8},{32,48},{40,56},{48,32},{56,40},{64,80... | collective-permute-start | bytes 393224 | tf_op jit(solution)/shard_map/ppermute | solution.py:24
  20.5 2.7 %collective-permute-start.11 = (bf16[4,16,1024]{2,1,0:T(8,128)(2,1)S(1)}, bf16[4,16,1024]{2,1,0:T(8,128)(2,1)S(1)}, u32[]{:S(2)}, u32[]{:S(2)}) collective-permute-start(bf16[4,16,1024]{2,1,0:T(8,128)(2,1)S(1)} %pad_maximum_fusion.1), channel_id=1, source_target_pairs={{0,32},{8,40},{16,48},{24,56},{32,0},{40,8},{48,16},{56,24},{64,96... | collective-permute-start | bytes 393224 | tf_op jit(solution)/shard_map/ppermute | solution.py:24
  23.2 0.5 collective-permute-start.12
  23.7 14.3 %collective-permute-done.2 = bf16[1,16,1024]{2,1,0:T(8,128)(2,1)S(1)} collective-permute-done((bf16[1,16,1024]{2,1,0:T(8,128)(2,1)S(1)}, bf16[1,16,1024]{2,1,0:T(8,128)(2,1)S(1)}, u32[]{:S(2)}, u32[]{:S(2)}) %collective-permute-start.2) | collective-permute-done | bytes 32800 | tf_op jit(solution)/shard_map/ppermute | solution.py:24
  38.1 1.6 %collective-permute-start.3 = (bf16[4,16,1024]{2,1,0:T(8,128)(2,1)S(1)}, bf16[4,16,1024]{2,1,0:T(8,128)(2,1)S(1)}, u32[]{:S(2)}, u32[]{:S(2)}) collective-permute-start(bf16[4,16,1024]{2,1,0:T(8,128)(2,1)S(1)} %pad_maximum_fusion), channel_id=1, source_target_pairs={{0,16},{8,24},{16,0},{24,8},{32,48},{40,56},{48,32},{56,40},{64,80... | collective-permute-start | bytes 393224 | tf_op jit(solution)/shard_map/ppermute | solution.py:24
  39.7 2.7 %collective-permute-start.4 = (bf16[4,16,1024]{2,1,0:T(8,128)(2,1)S(1)}, bf16[4,16,1024]{2,1,0:T(8,128)(2,1)S(1)}, u32[]{:S(2)}, u32[]{:S(2)}) collective-permute-start(bf16[4,16,1024]{2,1,0:T(8,128)(2,1)S(1)} %pad_maximum_fusion), channel_id=1, source_target_pairs={{0,32},{8,40},{16,48},{24,56},{32,0},{40,8},{48,16},{56,24},{64,96... | collective-permute-start | bytes 393224 | tf_op jit(solution)/shard_map/ppermute | solution.py:24
  42.4 0.6 collective-permute-start.5
  43.2 1.1 collective-permute-done.3
  44.3 3.7 %collective-permute-done.4 = bf16[4,16,1024]{2,1,0:T(8,128)(2,1)S(1)} collective-permute-done((bf16[4,16,1024]{2,1,0:T(8,128)(2,1)S(1)}, bf16[4,16,1024]{2,1,0:T(8,128)(2,1)S(1)}, u32[]{:S(2)}, u32[]{:S(2)}) %collective-permute-start.4) | collective-permute-done | bytes 131104 | tf_op jit(solution)/shard_map/ppermute | solution.py:24
  48.0 1.9 %collective-permute-done.5 = bf16[4,16,1024]{2,1,0:T(8,128)(2,1)S(1)} collective-permute-done((bf16[4,16,1024]{2,1,0:T(8,128)(2,1)S(1)}, bf16[4,16,1024]{2,1,0:T(8,128)(2,1)S(1)}, u32[]{:S(2)}, u32[]{:S(2)}) %collective-permute-start.5) | collective-permute-done | bytes 131104 | tf_op jit(solution)/shard_map/ppermute | solution.py:24
  50.1 0.7 copy.12.bias_ref
  50.8 0.8 copy-done.4
  51.6 1.0 copy-done.5
  52.7 0.7 copy-done.10
  53.4 1.7 %shard_map.102 = (bf16[512,1024]{1,0:T(8,128)(2,1)S(1)}, bf16[288,512]{1,0:T(8,128)(2,1)S(1)}, f32[32,512]{1,0:T(8,128)S(1)}, f32[32,512]{1,0:T(8,128)S(1)}, f32[8,128]{1,0:T(8,128)S(1)}) custom-call(s32[2]{0:T(128)S(1)} %pad_add_fusion.me_ref, bf16[16,16,1024]{2,1,0:T(8,128)(2,1)S(1)} %constant_dynamic-update-slice_fusion.7.near_ref, ...), custom_call_target="tpu_custom_call" | custom-call | flops 301989888 | bytes 4194304 | tf_op jit(solution)/shard_map/pallas_call | solution.py:191
  55.1 0.6 copy-done.8
  55.7 2.4 %shard_map.103 = (bf16[512,1024]{1,0:T(8,128)(2,1)S(1)}, f32[288,256]{1,0:T(8,128)S(1)}, bf16[288,256]{1,0:T(8,128)(2,1)}, bf16[288,256]{1,0:T(8,128)(2,1)}, bf16[288,256]{1,0:T(8,128)(2,1)}) custom-call(s32[2]{0:T(128)S(1)} %pad_add_fusion.me_ref, bf16[16,16,1024]{2,1,0:T(8,128)(2,1)S(1)} %constant_dynamic-update-slice_fusion.near_ref, ...), custom_call_target="tpu_custom_call" | custom-call | flops 301989888 | bytes 4194304 | tf_op jit(solution)/shard_map/pallas_call | solution.py:198
  58.2 1.0 copy-done.1
  59.1 0.7 copy-done.6
  59.8 0.5 copy-done.11
  60.3 1.5 %collective-permute-start.28 = (bf16[288,256]{1,0:T(8,128)(2,1)}, bf16[288,256]{1,0:T(8,128)(2,1)}, u32[]{:S(2)}, u32[]{:S(2)}) collective-permute-start(bf16[288,256]{1,0:T(8,128)(2,1)} %get-tuple-element.34), channel_id=1, source_target_pairs={{0,2},{1,3},{2,0},{3,1},{4,6},{5,7},{6,4},{7,5},{8,10},{9,11},{10,... | collective-permute-start | bytes 442376 | tf_op jit(solution)/shard_map/ppermute | solution.py:24
  61.8 2.7 %collective-permute-start.29 = (bf16[288,256]{1,0:T(8,128)(2,1)}, bf16[288,256]{1,0:T(8,128)(2,1)}, u32[]{:S(2)}, u32[]{:S(2)}) collective-permute-start(bf16[288,256]{1,0:T(8,128)(2,1)} %get-tuple-element.35), channel_id=1, source_target_pairs={{0,4},{1,5},{2,6},{3,7},{4,0},{5,1},{6,2},{7,3},{8,12},{9,13},{10,... | collective-permute-start | bytes 442376 | tf_op jit(solution)/shard_map/ppermute | solution.py:24
  64.6 0.5 collective-permute-start.30
  65.1 1.2 copy-done.2
  66.3 0.8 copy-done.9
  67.1 0.7 copy-done.12
  67.8 0.7 copy-done.15
  68.5 4.1 %shard_map.104 = (f32[256,1024]{1,0:T(8,128)S(1)}, f32[256,1024]{1,0:T(8,128)}, f32[304,256]{1,0:T(8,128)S(1)}, bf16[304,256]{1,0:T(8,128)(2,1)S(1)}, bf16[304,2...) custom-call(s32[2]{0:T(128)S(1)} %copy-done.12, bf16[32,32,384]{2,1,0:T(8,128)(2,1)S(1)} %all-to-all-done.w2_ref, ...), custom_call_target="tpu_custom_call" | custom-call | flops 905969664 | bytes 4194304 | tf_op jit(solution)/shard_map/pallas_call | solution.py:202
  72.6 0.3 collective-permute-start.21
  72.9 3.9 %collective-permute-start.22 = (bf16[304,256]{1,0:T(8,128)(2,1)S(1)}, bf16[304,256]{1,0:T(8,128)(2,1)S(1)}, u32[]{:S(2)}, u32[]{:S(2)}) collective-permute-start(bf16[304,256]{1,0:T(8,128)(2,1)S(1)} %get-tuple-element.31), channel_id=1, source_target_pairs={{0,4},{1,5},{2,6},{3,7},{4,0},{5,1},{6,2},{7,3},{8,12},{9,13},{10,... | collective-permute-start | bytes 466952 | tf_op jit(solution)/shard_map/ppermute | solution.py:24
  76.8 0.5 collective-permute-start.23
  77.3 1.1 add_convert_fusion.3
  78.4 5.9 %collective-permute-start.31 = (bf16[288,256]{1,0:T(8,128)(2,1)S(1)}, bf16[288,256]{1,0:T(8,128)(2,1)S(1)}, u32[]{:S(2)}, u32[]{:S(2)}) collective-permute-start(bf16[288,256]{1,0:T(8,128)(2,1)S(1)} %add_convert_fusion.3), channel_id=1, source_target_pairs={{0,1},{1,0},{2,3},{3,2},{4,5},{5,4},{6,7},{7,6},{8,9},{9,8},{10,11... | collective-permute-start | bytes 442376 | tf_op jit(solution)/shard_map/ppermute | solution.py:24
  84.3 1.7 %collective-permute-done.23 = bf16[304,256]{1,0:T(8,128)(2,1)S(1)} collective-permute-done((bf16[304,256]{1,0:T(8,128)(2,1)S(1)}, bf16[304,256]{1,0:T(8,128)(2,1)S(1)}, u32[]{:S(2)}, u32[]{:S(2)}) %collective-permute-start.23) | collective-permute-done | bytes 155680 | tf_op jit(solution)/shard_map/ppermute | solution.py:24
  86.1 5.9 %collective-permute-start.24 = (bf16[304,256]{1,0:T(8,128)(2,1)S(1)}, bf16[304,256]{1,0:T(8,128)(2,1)S(1)}, u32[]{:S(2)}, u32[]{:S(2)}) collective-permute-start(bf16[304,256]{1,0:T(8,128)(2,1)S(1)} %add_convert_fusion.1), channel_id=1, source_target_pairs={{0,1},{1,0},{2,3},{3,2},{4,5},{5,4},{6,7},{7,6},{8,9},{9,8},{10,11... | collective-permute-start | bytes 466952 | tf_op jit(solution)/shard_map/ppermute | solution.py:24
  92.1 2.2 %collective-permute-start.33 = (bf16[288,256]{1,0:T(8,128)(2,1)S(1)}, bf16[288,256]{1,0:T(8,128)(2,1)S(1)}, u32[]{:S(2)}, u32[]{:S(2)}) collective-permute-start(bf16[288,256]{1,0:T(8,128)(2,1)S(1)} %add_convert_fusion.2.a0), channel_id=1, source_target_pairs={{0,4},{1,5},{2,6},{3,7},{4,0},{5,1},{6,2},{7,3},{8,12},{9,13},{10,... | collective-permute-start | bytes 442376 | tf_op jit(solution)/shard_map/ppermute | solution.py:24
  94.3 2.5 %collective-permute-start.34 = (bf16[288,256]{1,0:T(8,128)(2,1)S(1)}, bf16[288,256]{1,0:T(8,128)(2,1)S(1)}, u32[]{:S(2)}, u32[]{:S(2)}) collective-permute-start(bf16[288,256]{1,0:T(8,128)(2,1)S(1)} %add_convert_fusion.2.a0), channel_id=1, source_target_pairs={{0,6},{1,7},{2,4},{3,5},{4,2},{5,3},{6,0},{7,1},{8,14},{9,15},{10,... | collective-permute-start | bytes 442376 | tf_op jit(solution)/shard_map/ppermute | solution.py:24
  96.8 1.4 %collective-permute-done.32.a1 = bf16[288,256]{1,0:T(8,128)(2,1)S(1)} collective-permute-done((bf16[288,256]{1,0:T(8,128)(2,1)S(1)}, bf16[288,256]{1,0:T(8,128)(2,1)S(1)}, u32[]{:S(2)}, u32[]{:S(2)}) %collective-permute-start.32) | collective-permute-done | bytes 147488 | tf_op jit(solution)/shard_map/ppermute | solution.py:24
  98.3 1.7 %collective-permute-done.33.a2 = bf16[288,256]{1,0:T(8,128)(2,1)S(1)} collective-permute-done((bf16[288,256]{1,0:T(8,128)(2,1)S(1)}, bf16[288,256]{1,0:T(8,128)(2,1)S(1)}, u32[]{:S(2)}, u32[]{:S(2)}) %collective-permute-start.33) | collective-permute-done | bytes 147488 | tf_op jit(solution)/shard_map/ppermute | solution.py:24
  100.0 1.6 %collective-permute-done.34.a3 = bf16[288,256]{1,0:T(8,128)(2,1)S(1)} collective-permute-done((bf16[288,256]{1,0:T(8,128)(2,1)S(1)}, bf16[288,256]{1,0:T(8,128)(2,1)S(1)}, u32[]{:S(2)}, u32[]{:S(2)}) %collective-permute-start.34) | collective-permute-done | bytes 147488 | tf_op jit(solution)/shard_map/ppermute | solution.py:24
  101.6 1.6 %shard_map.106 = f32[288,1024]{1,0:T(8,128)} custom-call(s32[2]{0:T(128)S(1)} %copy-done.13, bf16[288,256]{1,0:T(8,128)(2,1)S(1)} %add_convert_fusion.2.a0, bf16[288,256]{1,0:T(8,128)(2,1)S(1)} %collective-permute-done.32.a1, bf16[288,256]{1,0:T(8,128)(2,1)S(1)} %collective-permute-done.33.a2, bf16[288,256]{1,0:T(8,128)(2,1)S(1)} %collective-permute-done.34.a3), custom_call_target="tpu_custom_call" | custom-call | bytes 4194304 | tf_op jit(solution)/shard_map/pallas_call | solution.py:218
  103.3 2.8 %collective-permute-start.27 = (bf16[304,256]{1,0:T(8,128)(2,1)S(1)}, bf16[304,256]{1,0:T(8,128)(2,1)S(1)}, u32[]{:S(2)}, u32[]{:S(2)}) collective-permute-start(bf16[304,256]{1,0:T(8,128)(2,1)S(1)} %add_convert_fusion.a0), channel_id=1, source_target_pairs={{0,6},{1,7},{2,4},{3,5},{4,2},{5,3},{6,0},{7,1},{8,14},{9,15},{10,... | collective-permute-start | bytes 466952 | tf_op jit(solution)/shard_map/ppermute | solution.py:24
  106.1 1.4 %collective-permute-start.25 = (bf16[304,256]{1,0:T(8,128)(2,1)S(1)}, bf16[304,256]{1,0:T(8,128)(2,1)S(1)}, u32[]{:S(2)}, u32[]{:S(2)}) collective-permute-start(bf16[304,256]{1,0:T(8,128)(2,1)S(1)} %add_convert_fusion.a0), channel_id=1, source_target_pairs={{0,2},{1,3},{2,0},{3,1},{4,6},{5,7},{6,4},{7,5},{8,10},{9,11},{10,... | collective-permute-start | bytes 466952 | tf_op jit(solution)/shard_map/ppermute | solution.py:24
  107.5 4.3 %collective-permute-done.27.a3 = bf16[304,256]{1,0:T(8,128)(2,1)S(1)} collective-permute-done((bf16[304,256]{1,0:T(8,128)(2,1)S(1)}, bf16[304,256]{1,0:T(8,128)(2,1)S(1)}, u32[]{:S(2)}, u32[]{:S(2)}) %collective-permute-start.27) | collective-permute-done | bytes 155680 | tf_op jit(solution)/shard_map/ppermute | solution.py:24
  111.7 1.8 %collective-permute-done.26.a2 = bf16[304,256]{1,0:T(8,128)(2,1)S(1)} collective-permute-done((bf16[304,256]{1,0:T(8,128)(2,1)S(1)}, bf16[304,256]{1,0:T(8,128)(2,1)S(1)}, u32[]{:S(2)}, u32[]{:S(2)}) %collective-permute-start.26) | collective-permute-done | bytes 155680 | tf_op jit(solution)/shard_map/ppermute | solution.py:24
  113.9 2.6 %collective-permute-start.16 = (bf16[64,1024]{1,0:T(8,128)(2,1)S(1)}, bf16[64,1024]{1,0:T(8,128)(2,1)S(1)}, u32[]{:S(2)}, u32[]{:S(2)}) collective-permute-start(bf16[64,1024]{1,0:T(8,128)(2,1)S(1)} %get-tuple-element.41), channel_id=1, source_target_pairs={{0,32},{8,40},{16,48},{24,56},{32,0},{40,8},{48,16},{56,24},{64,96... | collective-permute-start | bytes 393224 | tf_op jit(solution)/shard_map/ppermute | solution.py:24
  116.5 2.1 %collective-permute-start.17 = (bf16[64,1024]{1,0:T(8,128)(2,1)S(1)}, bf16[64,1024]{1,0:T(8,128)(2,1)S(1)}, u32[]{:S(2)}, u32[]{:S(2)}) collective-permute-start(bf16[64,1024]{1,0:T(8,128)(2,1)S(1)} %get-tuple-element.40), channel_id=1, source_target_pairs={{0,48},{8,56},{16,32},{24,40},{32,16},{40,24},{48,0},{56,8},{64,11... | collective-permute-start | bytes 393224 | tf_op jit(solution)/shard_map/ppermute | solution.py:24
  118.9 2.0 %collective-permute-done.16 = bf16[64,1024]{1,0:T(8,128)(2,1)S(1)} collective-permute-done((bf16[64,1024]{1,0:T(8,128)(2,1)S(1)}, bf16[64,1024]{1,0:T(8,128)(2,1)S(1)}, u32[]{:S(2)}, u32[]{:S(2)}) %collective-permute-start.16) | collective-permute-done | bytes 131104 | tf_op jit(solution)/shard_map/ppermute | solution.py:24
  120.9 1.8 %collective-permute-done.17 = bf16[64,1024]{1,0:T(8,128)(2,1)S(1)} collective-permute-done((bf16[64,1024]{1,0:T(8,128)(2,1)S(1)}, bf16[64,1024]{1,0:T(8,128)(2,1)S(1)}, u32[]{:S(2)}, u32[]{:S(2)}) %collective-permute-start.17) | collective-permute-done | bytes 131104 | tf_op jit(solution)/shard_map/ppermute | solution.py:24
  122.9 2.5 %collective-permute-start.19 = (f32[16,1024]{1,0:T(8,128)S(1)}, f32[16,1024]{1,0:T(8,128)S(1)}, u32[]{:S(2)}, u32[]{:S(2)}) collective-permute-start(f32[16,1024]{1,0:T(8,128)S(1)} %get-tuple-element.44), channel_id=1, source_target_pairs={{0,128},{8,136},{16,144},{24,152},{32,160},{40,168},{48,176},{56,1... | collective-permute-start | bytes 196616 | tf_op jit(solution)/shard_map/ppermute | solution.py:24
  125.4 1.0 collective-permute-start.20
  126.4 0.5 add_bitcast_fusion
  126.9 1.6 %shard_map.105 = f32[288,1024]{1,0:T(8,128)} custom-call(s32[2]{0:T(128)S(1)} %copy-done.13, bf16[304,256]{1,0:T(8,128)(2,1)S(1)} %add_convert_fusion.a0, bf16[304,256]{1,0:T(8,128)(2,1)S(1)} %collective-permute-done.25.a1, bf16[304,256]{1,0:T(8,128)(2,1)S(1)} %collective-permute-done.26.a2, bf16[304,256]{1,0:T(8,128)(2,1)S(1)} %collective-permute-done.27.a3), custom_call_target="tpu_custom_call" | custom-call | bytes 4194304 | tf_op jit(solution)/shard_map/pallas_call | solution.py:219
  128.5 1.9 %collective-permute-done.20 = f32[16,1024]{1,0:T(8,128)S(1)} collective-permute-done((f32[16,1024]{1,0:T(8,128)S(1)}, f32[16,1024]{1,0:T(8,128)S(1)}, u32[]{:S(2)}, u32[]{:S(2)}) %collective-permute-start.20) | collective-permute-done | bytes 65568 | tf_op jit(solution)/shard_map/ppermute | solution.py:24
  130.4 0.6 fusion.6
  (90 shorter events, 1.6 us)
Async XLA Ops:
  0.6 16.7 %collective-permute-start.7 = (bf16[1,16,1024]{2,1,0:T(8,128)(2,1)}, bf16[1,16,1024]{2,1,0:T(8,128)(2,1)S(1)}, u32[]{:S(2)}, u32[]{:S(2)}) collective-permute-start(bf16[1,16,1024]{2,1,0:T(8,128)(2,1)} %bitcast.41), channel_id=1, source_target_pairs={{0,64},{8,72},{16,80},{24,88},{32,96},{40,104},{48,112},{56,120},{... | collective-permute-start | bytes 98312 | tf_op jit(solution)/shard_map/ppermute | solution.py:24
  2.6 16.3 %collective-permute-start.8 = (bf16[1,16,1024]{2,1,0:T(8,128)(2,1)}, bf16[1,16,1024]{2,1,0:T(8,128)(2,1)S(1)}, u32[]{:S(2)}, u32[]{:S(2)}) collective-permute-start(bf16[1,16,1024]{2,1,0:T(8,128)(2,1)} %bitcast.42), channel_id=1, source_target_pairs={{0,128},{8,136},{16,144},{24,152},{32,160},{40,168},{48,176},{56,1... | collective-permute-start | bytes 98312 | tf_op jit(solution)/shard_map/ppermute | solution.py:24
  4.1 14.8 %collective-permute-start.9 = (bf16[1,16,1024]{2,1,0:T(8,128)(2,1)}, bf16[1,16,1024]{2,1,0:T(8,128)(2,1)S(1)}, u32[]{:S(2)}, u32[]{:S(2)}) collective-permute-start(bf16[1,16,1024]{2,1,0:T(8,128)(2,1)} %bitcast.43), channel_id=1, source_target_pairs={{0,192},{8,200},{16,208},{24,216},{32,224},{40,232},{48,240},{56,2... | collective-permute-start | bytes 98312 | tf_op jit(solution)/shard_map/ppermute | solution.py:24
  4.6 18.6 %collective-permute-start = (bf16[1,16,1024]{2,1,0:T(8,128)(2,1)}, bf16[1,16,1024]{2,1,0:T(8,128)(2,1)S(1)}, u32[]{:S(2)}, u32[]{:S(2)}) collective-permute-start(bf16[1,16,1024]{2,1,0:T(8,128)(2,1)} %bitcast.37), channel_id=1, source_target_pairs={{0,64},{8,72},{16,80},{24,88},{32,96},{40,104},{48,112},{56,120},{... | collective-permute-start | bytes 98312 | tf_op jit(solution)/shard_map/ppermute | solution.py:24
  7.0 16.8 %collective-permute-start.1 = (bf16[1,16,1024]{2,1,0:T(8,128)(2,1)}, bf16[1,16,1024]{2,1,0:T(8,128)(2,1)S(1)}, u32[]{:S(2)}, u32[]{:S(2)}) collective-permute-start(bf16[1,16,1024]{2,1,0:T(8,128)(2,1)} %bitcast.38), channel_id=1, source_target_pairs={{0,128},{8,136},{16,144},{24,152},{32,160},{40,168},{48,176},{56,1... | collective-permute-start | bytes 98312 | tf_op jit(solution)/shard_map/ppermute | solution.py:24
  8.4 1.1 copy-start.3
  9.4 7.8 %copy-start.18 = (bf16[1,16,1,1024]{3,1,2,0:T(8,128)(2,1)S(1)}, bf16[1,16,1,1024]{3,1,2,0:T(8,128)(2,1)}, u32[]{:S(2)}) copy-start(bf16[1,16,1,1024]{3,1,2,0:T(8,128)(2,1)} %param.6) | copy-start | bytes 98308
  9.4 7.8 %copy-start.16 = (bf16[1,16,1,1024]{3,1,2,0:T(8,128)(2,1)S(1)}, bf16[1,16,1,1024]{3,1,2,0:T(8,128)(2,1)}, u32[]{:S(2)}) copy-start(bf16[1,16,1,1024]{3,1,2,0:T(8,128)(2,1)} %param.11) | copy-start | bytes 98308
  10.6 54.4 %all-to-all-start = ((bf16[32,32,384]{2,1,0:T(8,128)(2,1)}), bf16[32,32,384]{2,1,0:T(8,128)(2,1)S(1)}, u32[]{:S(2)}, u32[]{:S(2)}) async-start(bf16[32,32,384]{2,1,0:T(8,128)(2,1)} %bitcast.4), calls=%async_computation | async-start | bytes 1572864 | tf_op jit(solution)/shard_map/all_to_all | solution.py:189
  17.3 20.8 %collective-permute-start.2 = (bf16[1,16,1024]{2,1,0:T(8,128)(2,1)S(1)}, bf16[1,16,1024]{2,1,0:T(8,128)(2,1)S(1)}, u32[]{:S(2)}, u32[]{:S(2)}) collective-permute-start(bf16[1,16,1024]{2,1,0:T(8,128)(2,1)S(1)} %bitcast.39), channel_id=1, source_target_pairs={{0,192},{8,200},{16,208},{24,216},{32,224},{40,232},{48,240},{56,2... | collective-permute-start | bytes 98312 | tf_op jit(solution)/shard_map/ppermute | solution.py:24
  18.9 31.1 %copy-start.19 = (f32[32]{0:T(128)S(1)}, f32[32]{0:T(128)}, u32[]{:S(2)}) copy-start(f32[32]{0:T(128)} %param.9) | copy-start | bytes 388
  18.9 31.2 %copy-start.20 = (f32[32]{0:T(128)S(1)}, f32[32]{0:T(128)}, u32[]{:S(2)}) copy-start(f32[32]{0:T(128)} %param.10) | copy-start | bytes 388
  18.9 32.7 %copy-start = (bf16[9,32,1024]{2,1,0:T(8,128)(2,1)S(1)}, bf16[9,32,1024]{2,1,0:T(8,128)(2,1)}, u32[]{:S(2)}) copy-start(bf16[9,32,1024]{2,1,0:T(8,128)(2,1)} %param.7) | copy-start | bytes 1769476
  18.9 23.5 %collective-permute-start.10 = (bf16[4,16,1024]{2,1,0:T(8,128)(2,1)S(1)}, bf16[4,16,1024]{2,1,0:T(8,128)(2,1)S(1)}, u32[]{:S(2)}, u32[]{:S(2)}) collective-permute-start(bf16[4,16,1024]{2,1,0:T(8,128)(2,1)S(1)} %pad_maximum_fusion.1), channel_id=1, source_target_pairs={{0,16},{8,24},{16,0},{24,8},{32,48},{40,56},{48,32},{56,40},{64,80... | collective-permute-start | bytes 393224 | tf_op jit(solution)/shard_map/ppermute | solution.py:24
  20.5 22.6 %collective-permute-start.11 = (bf16[4,16,1024]{2,1,0:T(8,128)(2,1)S(1)}, bf16[4,16,1024]{2,1,0:T(8,128)(2,1)S(1)}, u32[]{:S(2)}, u32[]{:S(2)}) collective-permute-start(bf16[4,16,1024]{2,1,0:T(8,128)(2,1)S(1)} %pad_maximum_fusion.1), channel_id=1, source_target_pairs={{0,32},{8,40},{16,48},{24,56},{32,0},{40,8},{48,16},{56,24},{64,96... | collective-permute-start | bytes 393224 | tf_op jit(solution)/shard_map/ppermute | solution.py:24
  23.2 19.9 %collective-permute-start.12 = (bf16[4,16,1024]{2,1,0:T(8,128)(2,1)S(1)}, bf16[4,16,1024]{2,1,0:T(8,128)(2,1)S(1)}, u32[]{:S(2)}, u32[]{:S(2)}) collective-permute-start(bf16[4,16,1024]{2,1,0:T(8,128)(2,1)S(1)} %pad_maximum_fusion.1), channel_id=1, source_target_pairs={{0,48},{8,56},{16,32},{24,40},{32,16},{40,24},{48,0},{56,8},{64,11... | collective-permute-start | bytes 393224 | tf_op jit(solution)/shard_map/ppermute | solution.py:24
  38.1 6.2 %collective-permute-start.3 = (bf16[4,16,1024]{2,1,0:T(8,128)(2,1)S(1)}, bf16[4,16,1024]{2,1,0:T(8,128)(2,1)S(1)}, u32[]{:S(2)}, u32[]{:S(2)}) collective-permute-start(bf16[4,16,1024]{2,1,0:T(8,128)(2,1)S(1)} %pad_maximum_fusion), channel_id=1, source_target_pairs={{0,16},{8,24},{16,0},{24,8},{32,48},{40,56},{48,32},{56,40},{64,80... | collective-permute-start | bytes 393224 | tf_op jit(solution)/shard_map/ppermute | solution.py:24
  39.7 8.3 %collective-permute-start.4 = (bf16[4,16,1024]{2,1,0:T(8,128)(2,1)S(1)}, bf16[4,16,1024]{2,1,0:T(8,128)(2,1)S(1)}, u32[]{:S(2)}, u32[]{:S(2)}) collective-permute-start(bf16[4,16,1024]{2,1,0:T(8,128)(2,1)S(1)} %pad_maximum_fusion), channel_id=1, source_target_pairs={{0,32},{8,40},{16,48},{24,56},{32,0},{40,8},{48,16},{56,24},{64,96... | collective-permute-start | bytes 393224 | tf_op jit(solution)/shard_map/ppermute | solution.py:24
  42.4 7.4 %collective-permute-start.5 = (bf16[4,16,1024]{2,1,0:T(8,128)(2,1)S(1)}, bf16[4,16,1024]{2,1,0:T(8,128)(2,1)S(1)}, u32[]{:S(2)}, u32[]{:S(2)}) collective-permute-start(bf16[4,16,1024]{2,1,0:T(8,128)(2,1)S(1)} %pad_maximum_fusion), channel_id=1, source_target_pairs={{0,48},{8,56},{16,32},{24,40},{32,16},{40,24},{48,0},{56,8},{64,11... | collective-permute-start | bytes 393224 | tf_op jit(solution)/shard_map/ppermute | solution.py:24
  43.1 7.7 %collective-permute-start.13 = (bf16[16,16,1024]{2,1,0:T(8,128)(2,1)S(1)}, bf16[16,16,1024]{2,1,0:T(8,128)(2,1)S(1)}, u32[]{:S(2)}, u32[]{:S(2)}) collective-permute-start(bf16[16,16,1024]{2,1,0:T(8,128)(2,1)S(1)} %constant_dynamic-update-slice_fusion.7.near_ref), channel_id=1, source_target_pairs={{0,8},{8,0},{16,24},{24,16},{32,40},{40,32},{48,56},{56,48},{64,72... | collective-permute-start | bytes 1572872 | tf_op jit(solution)/shard_map/ppermute | solution.py:24
  49.9 5.9 %collective-permute-start.6 = (bf16[16,16,1024]{2,1,0:T(8,128)(2,1)S(1)}, bf16[16,16,1024]{2,1,0:T(8,128)(2,1)}, u32[]{:S(2)}, u32[]{:S(2)}) collective-permute-start(bf16[16,16,1024]{2,1,0:T(8,128)(2,1)S(1)} %constant_dynamic-update-slice_fusion.near_ref), channel_id=1, source_target_pairs={{0,8},{8,0},{16,24},{24,16},{32,40},{40,32},{48,56},{56,48},{64,72... | collective-permute-start | bytes 1572872 | tf_op jit(solution)/shard_map/ppermute | solution.py:24
  50.8 0.8 copy-start.4
  51.6 1.0 copy-start.5
  52.7 0.7 copy-start.10
  55.1 0.6 copy-start.8
  55.7 8.9 %copy-start.14 = (f32[8,128]{1,0:T(8,128)}, f32[8,128]{1,0:T(8,128)S(1)}, u32[]{:S(2)}) copy-start(f32[8,128]{1,0:T(8,128)S(1)} %get-tuple-element.26.rstd_ref) | copy-start | bytes 12292
  58.2 1.0 copy-start.1
  59.1 0.7 copy-start.6
  59.8 0.5 copy-start.11
  60.3 16.4 %collective-permute-start.28 = (bf16[288,256]{1,0:T(8,128)(2,1)}, bf16[288,256]{1,0:T(8,128)(2,1)}, u32[]{:S(2)}, u32[]{:S(2)}) collective-permute-start(bf16[288,256]{1,0:T(8,128)(2,1)} %get-tuple-element.34), channel_id=1, source_target_pairs={{0,2},{1,3},{2,0},{3,1},{4,6},{5,7},{6,4},{7,5},{8,10},{9,11},{10,... | collective-permute-start | bytes 442376 | tf_op jit(solution)/shard_map/ppermute | solution.py:24
  61.8 15.4 %collective-permute-start.29 = (bf16[288,256]{1,0:T(8,128)(2,1)}, bf16[288,256]{1,0:T(8,128)(2,1)}, u32[]{:S(2)}, u32[]{:S(2)}) collective-permute-start(bf16[288,256]{1,0:T(8,128)(2,1)} %get-tuple-element.35), channel_id=1, source_target_pairs={{0,4},{1,5},{2,6},{3,7},{4,0},{5,1},{6,2},{7,3},{8,12},{9,13},{10,... | collective-permute-start | bytes 442376 | tf_op jit(solution)/shard_map/ppermute | solution.py:24
  64.6 12.7 %collective-permute-start.30 = (bf16[288,256]{1,0:T(8,128)(2,1)}, bf16[288,256]{1,0:T(8,128)(2,1)}, u32[]{:S(2)}, u32[]{:S(2)}) collective-permute-start(bf16[288,256]{1,0:T(8,128)(2,1)} %get-tuple-element.36), channel_id=1, source_target_pairs={{0,6},{1,7},{2,4},{3,5},{4,2},{5,3},{6,0},{7,1},{8,14},{9,15},{10,... | collective-permute-start | bytes 442376 | tf_op jit(solution)/shard_map/ppermute | solution.py:24
  65.1 1.2 copy-start.2
  66.3 0.8 copy-start.9
  67.1 0.7 copy-start.12
  67.8 0.7 copy-start.15
  68.5 8.8 %copy-start.7 = (f32[288,256]{1,0:T(8,128)S(1)}, f32[288,256]{1,0:T(8,128)}, u32[]{:S(2)}) copy-start(f32[288,256]{1,0:T(8,128)} %copy-done.6) | copy-start | bytes 884740
  72.6 29.0 %copy-start.13 = (s32[2]{0:T(128)S(1)}, s32[2]{0:T(128)}, u32[]{:S(2)}) copy-start(s32[2]{0:T(128)} %copy-done.11) | copy-start | bytes 28
  72.6 11.8 %collective-permute-start.21 = (bf16[304,256]{1,0:T(8,128)(2,1)S(1)}, bf16[304,256]{1,0:T(8,128)(2,1)S(1)}, u32[]{:S(2)}, u32[]{:S(2)}) collective-permute-start(bf16[304,256]{1,0:T(8,128)(2,1)S(1)} %get-tuple-element.30), channel_id=1, source_target_pairs={{0,2},{1,3},{2,0},{3,1},{4,6},{5,7},{6,4},{7,5},{8,10},{9,11},{10,... | collective-permute-start | bytes 466952 | tf_op jit(solution)/shard_map/ppermute | solution.py:24
  72.9 11.5 %collective-permute-start.22 = (bf16[304,256]{1,0:T(8,128)(2,1)S(1)}, bf16[304,256]{1,0:T(8,128)(2,1)S(1)}, u32[]{:S(2)}, u32[]{:S(2)}) collective-permute-start(bf16[304,256]{1,0:T(8,128)(2,1)S(1)} %get-tuple-element.31), channel_id=1, source_target_pairs={{0,4},{1,5},{2,6},{3,7},{4,0},{5,1},{6,2},{7,3},{8,12},{9,13},{10,... | collective-permute-start | bytes 466952 | tf_op jit(solution)/shard_map/ppermute | solution.py:24
  76.8 9.2 %collective-permute-start.23 = (bf16[304,256]{1,0:T(8,128)(2,1)S(1)}, bf16[304,256]{1,0:T(8,128)(2,1)S(1)}, u32[]{:S(2)}, u32[]{:S(2)}) collective-permute-start(bf16[304,256]{1,0:T(8,128)(2,1)S(1)} %get-tuple-element.32), channel_id=1, source_target_pairs={{0,6},{1,7},{2,4},{3,5},{4,2},{5,3},{6,0},{7,1},{8,14},{9,15},{10,... | collective-permute-start | bytes 466952 | tf_op jit(solution)/shard_map/ppermute | solution.py:24
  78.4 13.6 %collective-permute-start.31 = (bf16[288,256]{1,0:T(8,128)(2,1)S(1)}, bf16[288,256]{1,0:T(8,128)(2,1)S(1)}, u32[]{:S(2)}, u32[]{:S(2)}) collective-permute-start(bf16[288,256]{1,0:T(8,128)(2,1)S(1)} %add_convert_fusion.3), channel_id=1, source_target_pairs={{0,1},{1,0},{2,3},{3,2},{4,5},{5,4},{6,7},{7,6},{8,9},{9,8},{10,11... | collective-permute-start | bytes 442376 | tf_op jit(solution)/shard_map/ppermute | solution.py:24
  86.1 17.2 %collective-permute-start.24 = (bf16[304,256]{1,0:T(8,128)(2,1)S(1)}, bf16[304,256]{1,0:T(8,128)(2,1)S(1)}, u32[]{:S(2)}, u32[]{:S(2)}) collective-permute-start(bf16[304,256]{1,0:T(8,128)(2,1)S(1)} %add_convert_fusion.1), channel_id=1, source_target_pairs={{0,1},{1,0},{2,3},{3,2},{4,5},{5,4},{6,7},{7,6},{8,9},{9,8},{10,11... | collective-permute-start | bytes 466952 | tf_op jit(solution)/shard_map/ppermute | solution.py:24
  92.0 6.2 %collective-permute-start.32 = (bf16[288,256]{1,0:T(8,128)(2,1)S(1)}, bf16[288,256]{1,0:T(8,128)(2,1)S(1)}, u32[]{:S(2)}, u32[]{:S(2)}) collective-permute-start(bf16[288,256]{1,0:T(8,128)(2,1)S(1)} %add_convert_fusion.2.a0), channel_id=1, source_target_pairs={{0,2},{1,3},{2,0},{3,1},{4,6},{5,7},{6,4},{7,5},{8,10},{9,11},{10,... | collective-permute-start | bytes 442376 | tf_op jit(solution)/shard_map/ppermute | solution.py:24
  92.1 7.8 %collective-permute-start.33 = (bf16[288,256]{1,0:T(8,128)(2,1)S(1)}, bf16[288,256]{1,0:T(8,128)(2,1)S(1)}, u32[]{:S(2)}, u32[]{:S(2)}) collective-permute-start(bf16[288,256]{1,0:T(8,128)(2,1)S(1)} %add_convert_fusion.2.a0), channel_id=1, source_target_pairs={{0,4},{1,5},{2,6},{3,7},{4,0},{5,1},{6,2},{7,3},{8,12},{9,13},{10,... | collective-permute-start | bytes 442376 | tf_op jit(solution)/shard_map/ppermute | solution.py:24
  94.3 7.3 %collective-permute-start.34 = (bf16[288,256]{1,0:T(8,128)(2,1)S(1)}, bf16[288,256]{1,0:T(8,128)(2,1)S(1)}, u32[]{:S(2)}, u32[]{:S(2)}) collective-permute-start(bf16[288,256]{1,0:T(8,128)(2,1)S(1)} %add_convert_fusion.2.a0), channel_id=1, source_target_pairs={{0,6},{1,7},{2,4},{3,5},{4,2},{5,3},{6,0},{7,1},{8,14},{9,15},{10,... | collective-permute-start | bytes 442376 | tf_op jit(solution)/shard_map/ppermute | solution.py:24
  96.8 16.8 %collective-permute-start.14 = (f32[256,1024]{1,0:T(8,128)}, f32[256,1024]{1,0:T(8,128)S(1)}, u32[]{:S(2)}, u32[]{:S(2)}) collective-permute-start(f32[256,1024]{1,0:T(8,128)} %get-tuple-element.28), channel_id=1, source_target_pairs={{0,8},{8,0},{16,24},{24,16},{32,40},{40,32},{48,56},{56,48},{64,72... | collective-permute-start | bytes 3145736 | tf_op jit(solution)/shard_map/ppermute | solution.py:24
  103.3 8.4 %collective-permute-start.27 = (bf16[304,256]{1,0:T(8,128)(2,1)S(1)}, bf16[304,256]{1,0:T(8,128)(2,1)S(1)}, u32[]{:S(2)}, u32[]{:S(2)}) collective-permute-start(bf16[304,256]{1,0:T(8,128)(2,1)S(1)} %add_convert_fusion.a0), channel_id=1, source_target_pairs={{0,6},{1,7},{2,4},{3,5},{4,2},{5,3},{6,0},{7,1},{8,14},{9,15},{10,... | collective-permute-start | bytes 466952 | tf_op jit(solution)/shard_map/ppermute | solution.py:24
  106.1 7.5 %collective-permute-start.26 = (bf16[304,256]{1,0:T(8,128)(2,1)S(1)}, bf16[304,256]{1,0:T(8,128)(2,1)S(1)}, u32[]{:S(2)}, u32[]{:S(2)}) collective-permute-start(bf16[304,256]{1,0:T(8,128)(2,1)S(1)} %add_convert_fusion.a0), channel_id=1, source_target_pairs={{0,4},{1,5},{2,6},{3,7},{4,0},{5,1},{6,2},{7,3},{8,12},{9,13},{10,... | collective-permute-start | bytes 466952 | tf_op jit(solution)/shard_map/ppermute | solution.py:24
  106.1 12.5 %collective-permute-start.25 = (bf16[304,256]{1,0:T(8,128)(2,1)S(1)}, bf16[304,256]{1,0:T(8,128)(2,1)S(1)}, u32[]{:S(2)}, u32[]{:S(2)}) collective-permute-start(bf16[304,256]{1,0:T(8,128)(2,1)S(1)} %add_convert_fusion.a0), channel_id=1, source_target_pairs={{0,2},{1,3},{2,0},{3,1},{4,6},{5,7},{6,4},{7,5},{8,10},{9,11},{10,... | collective-permute-start | bytes 466952 | tf_op jit(solution)/shard_map/ppermute | solution.py:24
  113.8 5.1 %collective-permute-start.15 = (bf16[64,1024]{1,0:T(8,128)(2,1)S(1)}, bf16[64,1024]{1,0:T(8,128)(2,1)S(1)}, u32[]{:S(2)}, u32[]{:S(2)}) collective-permute-start(bf16[64,1024]{1,0:T(8,128)(2,1)S(1)} %get-tuple-element.39), channel_id=1, source_target_pairs={{0,16},{8,24},{16,0},{24,8},{32,48},{40,56},{48,32},{56,40},{64,80... | collective-permute-start | bytes 393224 | tf_op jit(solution)/shard_map/ppermute | solution.py:24
  113.9 7.0 %collective-permute-start.16 = (bf16[64,1024]{1,0:T(8,128)(2,1)S(1)}, bf16[64,1024]{1,0:T(8,128)(2,1)S(1)}, u32[]{:S(2)}, u32[]{:S(2)}) collective-permute-start(bf16[64,1024]{1,0:T(8,128)(2,1)S(1)} %get-tuple-element.41), channel_id=1, source_target_pairs={{0,32},{8,40},{16,48},{24,56},{32,0},{40,8},{48,16},{56,24},{64,96... | collective-permute-start | bytes 393224 | tf_op jit(solution)/shard_map/ppermute | solution.py:24
  116.5 6.2 %collective-permute-start.17 = (bf16[64,1024]{1,0:T(8,128)(2,1)S(1)}, bf16[64,1024]{1,0:T(8,128)(2,1)S(1)}, u32[]{:S(2)}, u32[]{:S(2)}) collective-permute-start(bf16[64,1024]{1,0:T(8,128)(2,1)S(1)} %get-tuple-element.40), channel_id=1, source_target_pairs={{0,48},{8,56},{16,32},{24,40},{32,16},{40,24},{48,0},{56,8},{64,11... | collective-permute-start | bytes 393224 | tf_op jit(solution)/shard_map/ppermute | solution.py:24
  122.8 7.7 %copy-start.17 = (bf16[1,16,1,1024]{3,1,2,0:T(8,128)(2,1)S(1)}, bf16[1,16,1,1024]{3,1,2,0:T(8,128)(2,1)}, u32[]{:S(2)}) copy-start(bf16[1,16,1,1024]{3,1,2,0:T(8,128)(2,1)} %param.11) | copy-start | bytes 98308
  122.8 5.7 %collective-permute-start.18 = (f32[16,1024]{1,0:T(8,128)S(1)}, f32[16,1024]{1,0:T(8,128)S(1)}, u32[]{:S(2)}, u32[]{:S(2)}) collective-permute-start(f32[16,1024]{1,0:T(8,128)S(1)} %get-tuple-element.42), channel_id=1, source_target_pairs={{0,64},{8,72},{16,80},{24,88},{32,96},{40,104},{48,112},{56,120},{... | collective-permute-start | bytes 196616 | tf_op jit(solution)/shard_map/ppermute | solution.py:24
  122.9 5.6 %collective-permute-start.19 = (f32[16,1024]{1,0:T(8,128)S(1)}, f32[16,1024]{1,0:T(8,128)S(1)}, u32[]{:S(2)}, u32[]{:S(2)}) collective-permute-start(f32[16,1024]{1,0:T(8,128)S(1)} %get-tuple-element.44), channel_id=1, source_target_pairs={{0,128},{8,136},{16,144},{24,152},{32,160},{40,168},{48,176},{56,1... | collective-permute-start | bytes 196616 | tf_op jit(solution)/shard_map/ppermute | solution.py:24
  125.4 5.0 %collective-permute-start.20 = (f32[16,1024]{1,0:T(8,128)S(1)}, f32[16,1024]{1,0:T(8,128)S(1)}, u32[]{:S(2)}, u32[]{:S(2)}) collective-permute-start(f32[16,1024]{1,0:T(8,128)S(1)} %get-tuple-element.43), channel_id=1, source_target_pairs={{0,192},{8,200},{16,208},{24,216},{32,224},{40,232},{48,240},{56,2... | collective-permute-start | bytes 196616 | tf_op jit(solution)/shard_map/ppermute | solution.py:24
